TPU v7x, 256 devices: a whole 4x4x8 slice. The times are simulated.
256 devices in a mesh: dp: 16 (over z, core), tensor: 16 (over x, y).
Axes of the slice: x: 4, y: 4, z: 8, core: 2. Of those that a mesh axis runs over, the one named last changes fastest.
Arguments:
- acts: bfloat16 [32768, 8192], P('dp', 'tensor'), may hold values from -6 to 6
- grads: bfloat16 [32768, 28672], P('dp', 'tensor'), may hold values from -6 to 6
- sketch: float32 [64, 28672], P(None, 'tensor'), may hold values from -6 to 6
- picks: int32 [32768], P('dp'), may hold values from 0 to 2047
Outputs:
- adapter_down_weight: float32 [64, 28672], P(None, 'tensor')
- adapter_up_weight: float32 [64, 8192], P(None, 'tensor')
Inputs may be any that keep to these rules, and one draw needn't show every extreme that they name: picks[t] is a row of the 2048 rows of token t's own block of the pool, the block of rows (t // 2048) * 2048 onwards.
All inputs are finite; a program needn't handle non-finite values.
Results may differ from a plain program's by a relative error of at most 0.0003.
Values sent between devices are 32-bit elements; how exact they have to be, the bound alone decides.
No kernel may reach another device: no remote copies, remote signals or barrier semaphores. Data moves between devices by JAX's collectives and lax.ppermute only.
A program may use at most 128 MiB of HBM per device.

v0:
```python
import math

import jax
import jax.numpy as jnp
from jax import lax
from jax.sharding import PartitionSpec as P

MODEL_WIDTH = 8192
ITERS = 2


def solve_lower(factor_low, rows_t):
    return lax.linalg.triangular_solve(factor_low, rows_t, left_side=True, lower=True)


def gram_of(rows_t):
    return jnp.dot(
        rows_t, rows_t.T, precision=lax.Precision.HIGHEST, preferred_element_type=jnp.float32
    )


def token_side(left_t, sampled):
    return lax.dot_general(
        left_t,
        sampled,
        (((1,), (1,)), ((), ())),
        precision=lax.Precision.HIGHEST,
        preferred_element_type=jnp.float32,
    )


def hidden_feature_factor(proj_t, sampled):
    return jnp.dot(
        proj_t, sampled, precision=lax.Precision.HIGHEST, preferred_element_type=jnp.float32
    )


def summed_tokens(partial_t):
    return lax.psum(partial_t, "tensor")


def feature_totals(partial_t):
    return lax.psum(partial_t, "dp")


def per_device(acts, grads, sketch, picks):
    sample_x = jnp.take(acts, picks, axis=0)
    sampled_gradient = jnp.take(grads, picks, axis=0)
    token_count_overall = picks.shape[0] * lax.axis_size("dp")
    range_t = feature_totals(
        hidden_feature_factor(summed_tokens(token_side(sketch, sampled_gradient)), sample_x)
    )

    def orthonormal(rows_t):
        gram = lax.psum(gram_of(rows_t), "tensor")
        return solve_lower(jnp.linalg.cholesky(gram), rows_t)

    for step in range(ITERS):
        basis_transposed = orthonormal(range_t)
        left_projector = summed_tokens(token_side(basis_transposed, sample_x))
        co_range = feature_totals(hidden_feature_factor(left_projector, sampled_gradient))
        right_t = orthonormal(co_range)
        right_proj = summed_tokens(token_side(right_t, sampled_gradient))
        range_t = feature_totals(hidden_feature_factor(right_proj, sample_x))
    basis_transposed = orthonormal(range_t)
    left_projector = summed_tokens(token_side(basis_transposed, sample_x))
    adapter_down_weight = feature_totals(
        hidden_feature_factor(left_projector, sampled_gradient)
    ) / math.sqrt(token_count_overall)
    adapter_up_weight = basis_transposed * math.sqrt(MODEL_WIDTH)
    return (adapter_down_weight, adapter_up_weight)


def solution(mesh):
    return jax.shard_map(
        per_device,
        mesh=mesh,
        in_specs=(P("dp", "tensor"), P("dp", "tensor"), P(None, "tensor"), P("dp")),
        out_specs=(P(None, "tensor"), P(None, "tensor")),
        check_vma=False,
    )
```

profile of v0, /device:TPU:1, one launch (start us, length us, event | category | flops | bytes accessed | tf_op | source)
XLA Modules:
  0.0 1764.6 jit_solution(1404442238591347279)
XLA Ops:
  8.8 18.6 %gather_fusion = bf16[2048,1792]{1,0:T(8,128)(2,1)} fusion(bf16[2048,1792]{1,0:T(8,128)(2,1)} %param.10, s32[2048]{0:T(1024)S(1)} %fusion.28), kind=kCustom, calls=%fused_computation | custom fusion | bytes 14688256 | tf_op jit(solution)/shard_map/jit(_take)/gather | solution.py:48
  41.2 9.2 gather_fusion.1
  53.2 87.6 %all-reduce.13.cloned.1.call-done = f32[64,2048]{0,1:T(8,128)} async-done(((f32[64,2048]{0,1:T(8,128)}), f32[64,2048]{0,1:T(8,128)}) %all-reduce.13.cloned.1.call-update) | async-done | bytes 524304 | tf_op jit(solution)/shard_map/psum | solution.py:39
  144.5 108.3 %all-reduce.15.cloned.1.call-done = f32[64,512]{1,0:T(8,128)} async-done(((f32[64,512]{1,0:T(8,128)}), f32[64,512]{1,0:T(8,128)}) %all-reduce.15.cloned.1.call-update) | async-done | bytes 131088 | tf_op jit(solution)/shard_map/psum | solution.py:43
  254.0 60.7 %psum.121 = f32[64,64]{0,1:T(8,128)S(1)} all-reduce(f32[64,64]{0,1:T(8,128)S(1)} %fusion.30), channel_id=1, replica_groups=mesh['dp'=16,'tensor'=16] {'tensor'}, use_global_device_ids=true, to_apply=%region_2.3 | all-reduce | flops 4096 | bytes 32768 | tf_op jit(solution)/shard_map/psum | solution.py:55
  332.6 103.7 %all-reduce.17.cloned.1.call-done = f32[64,2048]{1,0:T(8,128)} async-done(((f32[64,2048]{1,0:T(8,128)}), f32[64,2048]{1,0:T(8,128)}) %all-reduce.17.cloned.1.call-update) | async-done | bytes 524304 | tf_op jit(solution)/shard_map/psum | solution.py:39
  436.3 7.9 fusion.32
  444.3 109.1 %all-reduce.19.cloned.1.call-done = f32[64,1792]{1,0:T(8,128)} async-done(((f32[64,1792]{1,0:T(8,128)}), f32[64,1792]{1,0:T(8,128)}) %all-reduce.19.cloned.1.call-update) | async-done | bytes 458768 | tf_op jit(solution)/shard_map/psum | solution.py:43
  555.1 60.8 %psum.124 = f32[64,64]{0,1:T(8,128)S(1)} all-reduce(f32[64,64]{0,1:T(8,128)S(1)} %fusion.33), channel_id=1, replica_groups=mesh['dp'=16,'tensor'=16] {'tensor'}, use_global_device_ids=true, to_apply=%region_7.10 | all-reduce | flops 4096 | bytes 32768 | tf_op jit(solution)/shard_map/psum | solution.py:55
  629.7 10.6 fusion.34
  640.4 101.7 %all-reduce.21.cloned.1.call-done = f32[64,2048]{1,0:T(8,128)} async-done(((f32[64,2048]{1,0:T(8,128)}), f32[64,2048]{1,0:T(8,128)}) %all-reduce.21.cloned.1.call-update) | async-done | bytes 524304 | tf_op jit(solution)/shard_map/psum | solution.py:39
  745.7 108.3 %all-reduce.23.cloned.1.call-done = f32[64,512]{1,0:T(8,128)} async-done(((f32[64,512]{1,0:T(8,128)}), f32[64,512]{1,0:T(8,128)}) %all-reduce.23.cloned.1.call-update) | async-done | bytes 131088 | tf_op jit(solution)/shard_map/psum | solution.py:43
  855.3 60.1 %psum.127 = f32[64,64]{0,1:T(8,128)S(1)} all-reduce(f32[64,64]{0,1:T(8,128)S(1)} %fusion.36), channel_id=1, replica_groups=mesh['dp'=16,'tensor'=16] {'tensor'}, use_global_device_ids=true, to_apply=%region_10.14 | all-reduce | flops 4096 | bytes 32768 | tf_op jit(solution)/shard_map/psum | solution.py:55
  933.4 103.5 %all-reduce.25.cloned.1.call-done = f32[64,2048]{1,0:T(8,128)} async-done(((f32[64,2048]{1,0:T(8,128)}), f32[64,2048]{1,0:T(8,128)}) %all-reduce.25.cloned.1.call-update) | async-done | bytes 524304 | tf_op jit(solution)/shard_map/psum | solution.py:39
  1036.9 7.9 fusion.38
  1044.9 109.1 %all-reduce.27.cloned.1.call-done = f32[64,1792]{1,0:T(8,128)} async-done(((f32[64,1792]{1,0:T(8,128)}), f32[64,1792]{1,0:T(8,128)}) %all-reduce.27.cloned.1.call-update) | async-done | bytes 458768 | tf_op jit(solution)/shard_map/psum | solution.py:43
  1155.7 60.5 %psum.130 = f32[64,64]{0,1:T(8,128)S(1)} all-reduce(f32[64,64]{0,1:T(8,128)S(1)} %fusion.39), channel_id=1, replica_groups=mesh['dp'=16,'tensor'=16] {'tensor'}, use_global_device_ids=true, to_apply=%region_13.17 | all-reduce | flops 4096 | bytes 32768 | tf_op jit(solution)/shard_map/psum | solution.py:55
  1230.0 10.6 fusion.40
  1240.7 101.8 %all-reduce.29.cloned.1.call-done = f32[64,2048]{1,0:T(8,128)} async-done(((f32[64,2048]{1,0:T(8,128)}), f32[64,2048]{1,0:T(8,128)}) %all-reduce.29.cloned.1.call-update) | async-done | bytes 524304 | tf_op jit(solution)/shard_map/psum | solution.py:39
  1346.1 108.3 %all-reduce.31.cloned.1.call-done = f32[64,512]{1,0:T(8,128)} async-done(((f32[64,512]{1,0:T(8,128)}), f32[64,512]{1,0:T(8,128)}) %all-reduce.31.cloned.1.call-update) | async-done | bytes 131088 | tf_op jit(solution)/shard_map/psum | solution.py:43
  1455.6 60.4 %psum.133 = f32[64,64]{0,1:T(8,128)S(1)} all-reduce(f32[64,64]{0,1:T(8,128)S(1)} %fusion.42), channel_id=1, replica_groups=mesh['dp'=16,'tensor'=16] {'tensor'}, use_global_device_ids=true, to_apply=%region_16.20 | all-reduce | flops 4096 | bytes 32768 | tf_op jit(solution)/shard_map/psum | solution.py:55
  1534.6 103.8 %all-reduce.33.cloned.1.call-done = f32[64,2048]{1,0:T(8,128)} async-done(((f32[64,2048]{1,0:T(8,128)}), f32[64,2048]{1,0:T(8,128)}) %all-reduce.33.cloned.1.call-update) | async-done | bytes 524304 | tf_op jit(solution)/shard_map/psum | solution.py:39
  1638.4 7.9 fusion.44
  1646.4 109.2 %all-reduce.35.cloned.1.call-done = f32[64,1792]{1,0:T(8,128)} async-done(((f32[64,1792]{1,0:T(8,128)}), f32[64,1792]{1,0:T(8,128)}) %all-reduce.35.cloned.1.call-update) | async-done | bytes 458768 | tf_op jit(solution)/shard_map/psum | solution.py:43
  (87 shorter events, 120.2 us)
Async XLA Ops:
  7.2 34.1 %copy-start = (bf16[2048,512]{1,0:T(8,128)(2,1)S(1)}, bf16[2048,512]{1,0:T(8,128)(2,1)}, u32[]{:S(2)}) copy-start(bf16[2048,512]{1,0:T(8,128)(2,1)} %param.9) | copy-start | bytes 6291460
  7.2 133.6 %all-reduce.13.cloned.1.call-start = ((), (), s32[]{:S(2)}) async-start(), calls=%async_computation | async-start | bytes 2097152 | tf_op jit(solution)/shard_map/psum | solution.py:39
  27.4 6.9 copy-start.2
  31.3 3.0 copy-start.1
  41.2 211.6 %all-reduce.15.cloned.1.call-start = ((), (), s32[]{:S(2)}) async-start(), calls=%async_computation.1 | async-start | bytes 262144 | tf_op jit(solution)/shard_map/psum | solution.py:43
  144.4 291.9 %all-reduce.17.cloned.1.call-start = ((), (), s32[]{:S(2)}) async-start(), calls=%async_computation.2 | async-start | bytes 1048576 | tf_op jit(solution)/shard_map/psum | solution.py:39
  332.6 220.9 %all-reduce.19.cloned.1.call-start = ((), (), s32[]{:S(2)}) async-start(), calls=%async_computation.3 | async-start | bytes 917504 | tf_op jit(solution)/shard_map/psum | solution.py:43
  444.3 297.8 %all-reduce.21.cloned.1.call-start = ((), (), s32[]{:S(2)}) async-start(), calls=%async_computation.4 | async-start | bytes 1048576 | tf_op jit(solution)/shard_map/psum | solution.py:39
  640.3 213.7 %all-reduce.23.cloned.1.call-start = ((), (), s32[]{:S(2)}) async-start(), calls=%async_computation.5 | async-start | bytes 262144 | tf_op jit(solution)/shard_map/psum | solution.py:43
  745.7 291.2 %all-reduce.25.cloned.1.call-start = ((), (), s32[]{:S(2)}) async-start(), calls=%async_computation.6 | async-start | bytes 1048576 | tf_op jit(solution)/shard_map/psum | solution.py:39
  933.2 220.8 %all-reduce.27.cloned.1.call-start = ((), (), s32[]{:S(2)}) async-start(), calls=%async_computation.7 | async-start | bytes 917504 | tf_op jit(solution)/shard_map/psum | solution.py:43
  1044.8 297.6 %all-reduce.29.cloned.1.call-start = ((), (), s32[]{:S(2)}) async-start(), calls=%async_computation.8 | async-start | bytes 1048576 | tf_op jit(solution)/shard_map/psum | solution.py:39
  1240.6 213.8 %all-reduce.31.cloned.1.call-start = ((), (), s32[]{:S(2)}) async-start(), calls=%async_computation.9 | async-start | bytes 262144 | tf_op jit(solution)/shard_map/psum | solution.py:43
  1346.0 292.4 %all-reduce.33.cloned.1.call-start = ((), (), s32[]{:S(2)}) async-start(), calls=%async_computation.10 | async-start | bytes 1048576 | tf_op jit(solution)/shard_map/psum | solution.py:39
  1534.5 221.0 %all-reduce.35.cloned.1.call-start = ((), (), s32[]{:S(2)}) async-start(), calls=%async_computation.11 | async-start | bytes 917504 | tf_op jit(solution)/shard_map/psum | solution.py:43
Sparse Core Ops, SparseCore 0:
  41.3 99.4 all-reduce.12
  144.5 108.2 all-reduce.14
  332.7 103.5 all-reduce.16
  444.4 109.0 all-reduce.18
  640.4 101.5 all-reduce.20
  745.8 108.1 all-reduce.22
  933.3 103.5 all-reduce.24
  1045.0 109.0 all-reduce.26
  1240.7 101.6 all-reduce.28
  1346.2 108.1 all-reduce.30
  1534.7 103.7 all-reduce.32
  1646.5 109.0 all-reduce.34
where the time goes:
time: 1770 us; the launch traced here: 1760 us
  waiting for transfers between devices  1250 us (71%)
  blocking collectives  303 us (17%)
  matrix products  90.4 us (5%)
  other arithmetic  70.5 us (4%)
  local copies, waits for them, and re-layouts  31.1 us (2%)
    psum x6, waiting for transfers between devices, feature_totals(): return lax.psum(partial_t, 'dp')  652 us
    psum x6, waiting for transfers between devices, summed_tokens(): return lax.psum(partial_t, 'tensor')  602 us
    psum x5, blocking collectives, orthonormal(): gram = lax.psum(gram_of(rows_t), 'tensor')  303 us
    dot_general x6, matrix products, token_side(): lax.dot_general(left_t, sampled, (((1,), (1,)), ((), ())), precision=lax....  41.2 us
  transfers between devices with their start and end apart: 12, of which 12 were waited for; matrix products, arithmetic and copies ran while one was open for 1% of the time, Pallas kernels for 0%

commit v1 on v0

v1 whole, which is shorter than its diff:
```python
import math

import jax
import jax.numpy as jnp
from jax import lax
from jax.sharding import PartitionSpec as P

MODEL_WIDTH = 8192
ITERS = 2
R = 64
HIGH = lax.Precision.HIGHEST


def pieces(m):
    hi = lax.reduce_precision(m, 8, 7)
    rest = m - hi
    mid = lax.reduce_precision(rest, 8, 7)
    low = rest - mid
    return jnp.concatenate([hi, mid, low], axis=0).astype(jnp.bfloat16)


def whole(out):
    return out[:R] + (out[R : 2 * R] + out[2 * R :])


def times_transposed(m, w):
    return whole(
        lax.dot_general(
            pieces(m), w, (((1,), (1,)), ((), ())), preferred_element_type=jnp.float32
        )
    )


def times(m, w):
    return whole(jnp.dot(pieces(m), w, preferred_element_type=jnp.float32))


def counts_of(picks):
    tok = picks.shape[0]
    high_at = (picks[None, :] // 128 == jnp.arange(tok // 128, dtype=jnp.int32)[:, None])
    low_at = (picks[:, None] % 128 == jnp.arange(128, dtype=jnp.int32)[None, :])
    found = jnp.dot(
        high_at.astype(jnp.bfloat16),
        low_at.astype(jnp.bfloat16),
        preferred_element_type=jnp.float32,
    )
    return found.reshape(1, tok)


def tensor_sum(part):
    n = part.shape[0]
    mine = jnp.sum(lax.all_to_all(part, "tensor", 0, 0), axis=0)
    return lax.all_to_all(jnp.broadcast_to(mine[None], (n,) + mine.shape), "tensor", 0, 0)


def token_totals(m, w, with_gram):
    prod = times_transposed(m, w)
    n = prod.shape[1] // 128
    part = prod.reshape(R, n, 128).transpose(1, 0, 2)
    if with_gram:
        gram = jnp.dot(m, m.T, precision=HIGH, preferred_element_type=jnp.float32)
        gram = gram.reshape(n, R // n, R)
        gram = jnp.pad(gram, ((0, 0), (0, 8 - R // n), (0, 128 - R)))
        part = jnp.concatenate([part, gram], axis=1)
    total = tensor_sum(part)
    prod = total[:, :R].transpose(1, 0, 2).reshape(R, n * 128)
    if not with_gram:
        return prod, None
    return prod, total[:, R : R + R // n, :R].reshape(R, R)


def inverse_factor(gram):
    factor = jnp.linalg.cholesky(gram)
    eye = jnp.eye(R, dtype=jnp.float32)
    return lax.linalg.triangular_solve(factor, eye, left_side=True, lower=True)


def apply_left(factor, m):
    return jnp.dot(factor, m, precision=HIGH, preferred_element_type=jnp.float32)


def feature_totals(part):
    n = part.shape[1]
    size = lax.axis_size("dp")
    nz = size // 2
    swap = [(i, i ^ 1) for i in range(size)]
    groups = [[2 * z + c for z in range(nz)] for c in range(2)]
    core = lax.axis_index("dp") % 2
    blocks = part.reshape(2, R // 16, 8, 2, n // 2).transpose(0, 1, 3, 2, 4)
    blocks = blocks.reshape(2, nz, 8, n // 2)
    kept = lax.dynamic_index_in_dim(blocks, core, 0, keepdims=False)
    sent = lax.dynamic_index_in_dim(blocks, 1 - core, 0, keepdims=False)
    half = kept + lax.ppermute(sent, "dp", swap)
    own = jnp.sum(lax.all_to_all(half, "dp", 0, 0, axis_index_groups=groups), axis=0)
    half = lax.all_to_all(
        jnp.broadcast_to(own[None], (nz,) + own.shape), "dp", 0, 0, axis_index_groups=groups
    )
    other = lax.ppermute(half, "dp", swap)
    full = jnp.where(core == 0, jnp.stack([half, other]), jnp.stack([other, half]))
    return full.reshape(2, R // 16, 2, 8, n // 2).transpose(0, 1, 3, 2, 4).reshape(R, n)


def per_device(acts, grads, sketch, picks):
    token_count_overall = picks.shape[0] * lax.axis_size("dp")
    counts = counts_of(picks)
    proj, _ = token_totals(sketch, grads, False)
    range_t = feature_totals(times(proj * counts, acts))
    for step in range(ITERS):
        proj, gram = token_totals(range_t, acts, True)
        proj = apply_left(inverse_factor(gram), proj)
        co_range = feature_totals(times(proj * counts, grads))
        proj, gram = token_totals(co_range, grads, True)
        proj = apply_left(inverse_factor(gram), proj)
        range_t = feature_totals(times(proj * counts, acts))
    proj, gram = token_totals(range_t, acts, True)
    factor = inverse_factor(gram)
    proj = apply_left(factor, proj)
    adapter_down_weight = feature_totals(times(proj * counts, grads)) / math.sqrt(
        token_count_overall
    )
    adapter_up_weight = apply_left(factor, range_t) * math.sqrt(MODEL_WIDTH)
    return (adapter_down_weight, adapter_up_weight)


def solution(mesh):
    return jax.shard_map(
        per_device,
        mesh=mesh,
        in_specs=(P("dp", "tensor"), P("dp", "tensor"), P(None, "tensor"), P("dp")),
        out_specs=(P(None, "tensor"), P(None, "tensor")),
        check_vma=False,
    )
```

time: 1770 us -> 478 us (0.27)
  waiting for transfers between devices: 1250 us -> 19.8 us
  matrix products: 90.4 us -> 42.8 us
  starting transfers between devices: 0.71 us -> 35.8 us
  local copies, waits for them, and re-layouts: 31.1 us -> 3.69 us
    psum x12 -> x0, waiting for transfers between devices: 1250 us -> none  [the longest x6 652 us: feature_totals(): return lax.psum(partial_t, 'dp')]
    psum x5 -> x0, blocking collectives: 303 us -> none  [orthonormal(): gram = lax.psum(gram_of(rows_t), 'tensor')]
    all_to_all x0 -> x23, blocking collectives: none -> 300 us  [the longest x6 90 us: tensor_sum(): mine = jnp.sum(lax.all_to_all(part, 'tensor', 0, 0), axis=0)]
    dot_general x17 -> x24, matrix products: 82.8 us -> 41.5 us  [the longest x6 19.3 us: times_transposed(): lax.dot_general(pieces(m), w, (((1,), (1,)), ((), ())), preferred_element...]
    ppermute x0 -> x12, starting transfers between devices: none -> 32.2 us  [the longest x6 18.6 us: feature_totals(): half = kept + lax.ppermute(sent, 'dp', swap)]
    gather x2 -> x0, local copies, waits for them, and re-layouts: 27.8 us -> none  [the longest x1 18.6 us: per_device(): sampled_gradient = jnp.take(grads, picks, axis=0)]
    another operation x25 -> x32, other arithmetic: 60.3 us -> 62 us  [the longest x15 32.6 us: inverse_factor(): factor = jnp.linalg.cholesky(gram)]
  transfers between devices with their start and end apart: 12 -> 13, of which waited for: 12 -> 13; matrix products, arithmetic and copies ran while one was open for 1% -> 0% of each run, Pallas kernels for 0% -> 0%
where the time goes in v1:
time: 478 us; the launch traced here: 469 us
  blocking collectives  300 us (63%)
  other arithmetic  64.5 us (13%)
  matrix products  42.8 us (9%)
  starting transfers between devices  35.8 us (7%)
  waiting for transfers between devices  19.8 us (4%)
    all_to_all x6, blocking collectives, tensor_sum(): mine = jnp.sum(lax.all_to_all(part, 'tensor', 0, 0), axis=0)  90 us
    all_to_all x6, blocking collectives, feature_totals(): lax.all_to_all(half, 'dp', 0, 0, axis_index_groups=groups)  76.1 us
    all_to_all x6, blocking collectives, feature_totals(): lax.all_to_all(jnp.broadcast_to(own[None], (nz,) + own.shape), 'dp', 0, 0...  67.3 us
    all_to_all x5, blocking collectives, tensor_sum(): lax.all_to_all(jnp.broadcast_to(mine[None], (n,) + mine.shape), 'tensor',...  67 us
    another operation x15, other arithmetic, inverse_factor(): factor = jnp.linalg.cholesky(gram)  32.6 us
    another operation x10, other arithmetic, inverse_factor(): return lax.linalg.triangular_solve(factor, eye, left_side=True, lower=True)  27.7 us
    dot_general x6, matrix products, times_transposed(): lax.dot_general(pieces(m), w, (((1,), (1,)), ((), ())), preferred_element...  19.3 us
    ppermute x6, starting transfers between devices, feature_totals(): half = kept + lax.ppermute(sent, 'dp', swap)  18.6 us
  transfers between devices with their start and end apart: 13, of which 13 were waited for; matrix products, arithmetic and copies ran while one was open for 0% of the time, Pallas kernels for 0%

profile of v1, /device:TPU:1, one launch (start us, length us, event | category | flops | bytes accessed | tf_op | source)
XLA Modules:
  0.0 469.0 jit_solution(9161210776855511854)
XLA Ops:
  7.6 17.7 %all_to_all.120 = f32[16,64,128]{2,1,0:T(8,128)S(1)} all-to-all(f32[16,64,128]{2,1,0:T(8,128)S(1)} %bitcast_bitcast_fusion.5), channel_id=1, replica_groups=mesh['dp'=16,'tensor'=16] {'tensor'}, dimensions={0} | all-to-all | bytes 1048576 | tf_op jit(solution)/shard_map/all_to_all | solution.py:52
  30.3 8.7 %all-to-all-done.1 = f32[16,64,128]{2,1,0:T(8,128)S(1)} async-done(((f32[16,64,128]{2,1,0:T(8,128)}), f32[16,64,128]{2,1,0:T(8,128)S(1)}, u32[]{:S(2)}, u32[]{:S(2)}) %all-to-all-start.1) | async-done | bytes 524320 | tf_op jit(solution)/shard_map/all_to_all | solution.py:53
  44.0 15.2 %all_to_all.121 = f32[8,8,256]{2,1,0:T(8,128)S(1)} all-to-all(f32[8,8,256]{2,1,0:T(8,128)S(1)} %bitcast_add_fusion.5), channel_id=1, replica_groups={{0,32,64,96,128,160,192,224},{16,48,80,112,144,176,208,240},{1,33,65,97..., dimensions={0} | all-to-all | bytes 131072 | tf_op jit(solution)/shard_map/all_to_all | solution.py:94
  59.2 9.7 %all_to_all.122 = f32[8,8,256]{2,1,0:T(8,128)S(1)} all-to-all(f32[8,8,256]{2,1,0:T(8,128)S(1)} %broadcast_in_dim.26), channel_id=1, replica_groups={{0,32,64,96,128,160,192,224},{16,48,80,112,144,176,208,240},{1,33,65,97..., dimensions={0} | all-to-all | bytes 131072 | tf_op jit(solution)/shard_map/all_to_all | solution.py:95
  74.2 14.5 %all_to_all.123 = f32[16,72,128]{2,1,0:T(8,128)S(1)} all-to-all(f32[16,72,128]{2,1,0:T(8,128)S(1)} %select_maximum_fusion.4), channel_id=1, replica_groups=mesh['dp'=16,'tensor'=16] {'tensor'}, dimensions={0} | all-to-all | bytes 1179648 | tf_op jit(solution)/shard_map/all_to_all | solution.py:52
  88.8 13.4 %all_to_all.124 = f32[16,72,128]{2,1,0:T(8,128)S(1)} all-to-all(f32[16,72,128]{2,1,0:T(8,128)S(1)} %broadcast_in_dim.27), channel_id=1, replica_groups=mesh['dp'=16,'tensor'=16] {'tensor'}, dimensions={0} | all-to-all | bytes 1179648 | tf_op jit(solution)/shard_map/all_to_all | solution.py:53
  124.2 14.0 %all_to_all.125 = f32[8,8,896]{2,1,0:T(8,128)S(1)} all-to-all(f32[8,8,896]{2,1,0:T(8,128)S(1)} %bitcast_add_fusion.2), channel_id=1, replica_groups={{0,32,64,96,128,160,192,224},{16,48,80,112,144,176,208,240},{1,33,65,97..., dimensions={0} | all-to-all | bytes 458752 | tf_op jit(solution)/shard_map/all_to_all | solution.py:94
  138.2 12.8 %all_to_all.126 = f32[8,8,896]{2,1,0:T(8,128)S(1)} all-to-all(f32[8,8,896]{2,1,0:T(8,128)S(1)} %broadcast_in_dim.28), channel_id=1, replica_groups={{0,32,64,96,128,160,192,224},{16,48,80,112,144,176,208,240},{1,33,65,97..., dimensions={0} | all-to-all | bytes 458752 | tf_op jit(solution)/shard_map/all_to_all | solution.py:95
  161.2 14.4 %all_to_all.127 = f32[16,72,128]{2,1,0:T(8,128)S(1)} all-to-all(f32[16,72,128]{2,1,0:T(8,128)S(1)} %select_maximum_fusion.3), channel_id=1, replica_groups=mesh['dp'=16,'tensor'=16] {'tensor'}, dimensions={0} | all-to-all | bytes 1179648 | tf_op jit(solution)/shard_map/all_to_all | solution.py:52
  175.7 13.3 %all_to_all.128 = f32[16,72,128]{2,1,0:T(8,128)S(1)} all-to-all(f32[16,72,128]{2,1,0:T(8,128)S(1)} %broadcast_in_dim.29), channel_id=1, replica_groups=mesh['dp'=16,'tensor'=16] {'tensor'}, dimensions={0} | all-to-all | bytes 1179648 | tf_op jit(solution)/shard_map/all_to_all | solution.py:53
  206.7 9.5 %all_to_all.129 = f32[8,8,256]{2,1,0:T(8,128)S(1)} all-to-all(f32[8,8,256]{2,1,0:T(8,128)S(1)} %bitcast_add_fusion.4), channel_id=1, replica_groups={{0,32,64,96,128,160,192,224},{16,48,80,112,144,176,208,240},{1,33,65,97..., dimensions={0} | all-to-all | bytes 131072 | tf_op jit(solution)/shard_map/all_to_all | solution.py:94
  216.2 9.6 %all_to_all.130 = f32[8,8,256]{2,1,0:T(8,128)S(1)} all-to-all(f32[8,8,256]{2,1,0:T(8,128)S(1)} %broadcast_in_dim.30), channel_id=1, replica_groups={{0,32,64,96,128,160,192,224},{16,48,80,112,144,176,208,240},{1,33,65,97..., dimensions={0} | all-to-all | bytes 131072 | tf_op jit(solution)/shard_map/all_to_all | solution.py:95
  231.0 14.5 %all_to_all.131 = f32[16,72,128]{2,1,0:T(8,128)S(1)} all-to-all(f32[16,72,128]{2,1,0:T(8,128)S(1)} %select_maximum_fusion.2), channel_id=1, replica_groups=mesh['dp'=16,'tensor'=16] {'tensor'}, dimensions={0} | all-to-all | bytes 1179648 | tf_op jit(solution)/shard_map/all_to_all | solution.py:52
  245.6 13.6 %all_to_all.132 = f32[16,72,128]{2,1,0:T(8,128)S(1)} all-to-all(f32[16,72,128]{2,1,0:T(8,128)S(1)} %broadcast_in_dim.31), channel_id=1, replica_groups=mesh['dp'=16,'tensor'=16] {'tensor'}, dimensions={0} | all-to-all | bytes 1179648 | tf_op jit(solution)/shard_map/all_to_all | solution.py:53
  281.2 14.0 %all_to_all.133 = f32[8,8,896]{2,1,0:T(8,128)S(1)} all-to-all(f32[8,8,896]{2,1,0:T(8,128)S(1)} %bitcast_add_fusion.1), channel_id=1, replica_groups={{0,32,64,96,128,160,192,224},{16,48,80,112,144,176,208,240},{1,33,65,97..., dimensions={0} | all-to-all | bytes 458752 | tf_op jit(solution)/shard_map/all_to_all | solution.py:94
  295.2 12.8 %all_to_all.134 = f32[8,8,896]{2,1,0:T(8,128)S(1)} all-to-all(f32[8,8,896]{2,1,0:T(8,128)S(1)} %broadcast_in_dim.32), channel_id=1, replica_groups={{0,32,64,96,128,160,192,224},{16,48,80,112,144,176,208,240},{1,33,65,97..., dimensions={0} | all-to-all | bytes 458752 | tf_op jit(solution)/shard_map/all_to_all | solution.py:95
  318.0 14.4 %all_to_all.135 = f32[16,72,128]{2,1,0:T(8,128)S(1)} all-to-all(f32[16,72,128]{2,1,0:T(8,128)S(1)} %select_maximum_fusion.1), channel_id=1, replica_groups=mesh['dp'=16,'tensor'=16] {'tensor'}, dimensions={0} | all-to-all | bytes 1179648 | tf_op jit(solution)/shard_map/all_to_all | solution.py:52
  332.6 13.3 %all_to_all.136 = f32[16,72,128]{2,1,0:T(8,128)S(1)} all-to-all(f32[16,72,128]{2,1,0:T(8,128)S(1)} %broadcast_in_dim.33), channel_id=1, replica_groups=mesh['dp'=16,'tensor'=16] {'tensor'}, dimensions={0} | all-to-all | bytes 1179648 | tf_op jit(solution)/shard_map/all_to_all | solution.py:53
  363.8 9.5 %all_to_all.137 = f32[8,8,256]{2,1,0:T(8,128)S(1)} all-to-all(f32[8,8,256]{2,1,0:T(8,128)S(1)} %bitcast_add_fusion.3), channel_id=1, replica_groups={{0,32,64,96,128,160,192,224},{16,48,80,112,144,176,208,240},{1,33,65,97..., dimensions={0} | all-to-all | bytes 131072 | tf_op jit(solution)/shard_map/all_to_all | solution.py:94
  373.4 9.6 %all_to_all.138 = f32[8,8,256]{2,1,0:T(8,128)S(1)} all-to-all(f32[8,8,256]{2,1,0:T(8,128)S(1)} %broadcast_in_dim.34), channel_id=1, replica_groups={{0,32,64,96,128,160,192,224},{16,48,80,112,144,176,208,240},{1,33,65,97..., dimensions={0} | all-to-all | bytes 131072 | tf_op jit(solution)/shard_map/all_to_all | solution.py:95
  388.2 14.5 %all_to_all.139 = f32[16,72,128]{2,1,0:T(8,128)S(1)} all-to-all(f32[16,72,128]{2,1,0:T(8,128)S(1)} %select_maximum_fusion), channel_id=1, replica_groups=mesh['dp'=16,'tensor'=16] {'tensor'}, dimensions={0} | all-to-all | bytes 1179648 | tf_op jit(solution)/shard_map/all_to_all | solution.py:52
  402.7 13.4 %all_to_all.140 = f32[16,72,128]{2,1,0:T(8,128)S(1)} all-to-all(f32[16,72,128]{2,1,0:T(8,128)S(1)} %broadcast_in_dim.35), channel_id=1, replica_groups=mesh['dp'=16,'tensor'=16] {'tensor'}, dimensions={0} | all-to-all | bytes 1179648 | tf_op jit(solution)/shard_map/all_to_all | solution.py:53
  438.1 14.0 %all_to_all.141 = f32[8,8,896]{2,1,0:T(8,128)S(1)} all-to-all(f32[8,8,896]{2,1,0:T(8,128)S(1)} %bitcast_add_fusion), channel_id=1, replica_groups={{0,32,64,96,128,160,192,224},{16,48,80,112,144,176,208,240},{1,33,65,97..., dimensions={0} | all-to-all | bytes 458752 | tf_op jit(solution)/shard_map/all_to_all | solution.py:94
  452.1 12.8 %all_to_all.142 = f32[8,8,896]{2,1,0:T(8,128)S(1)} all-to-all(f32[8,8,896]{2,1,0:T(8,128)S(1)} %broadcast_in_dim.36), channel_id=1, replica_groups={{0,32,64,96,128,160,192,224},{16,48,80,112,144,176,208,240},{1,33,65,97..., dimensions={0} | all-to-all | bytes 458752 | tf_op jit(solution)/shard_map/all_to_all | solution.py:95
  (185 shorter events, 157.9 us)
Async XLA Ops:
  0.6 38.4 %copy-start = (bf16[2048,512]{1,0:T(8,128)(2,1)S(1)}, bf16[2048,512]{1,0:T(8,128)(2,1)}, u32[]{:S(2)}) copy-start(bf16[2048,512]{1,0:T(8,128)(2,1)} %param.7) | copy-start | bytes 6291460
  7.6 22.2 %copy-start.1 = (s32[2048]{0:T(1024)S(1)}, s32[2048]{0:T(1024)}, u32[]{:S(2)}) copy-start(s32[2048]{0:T(1024)} %param.10) | copy-start | bytes 24580
  26.2 12.7 %all-to-all-start.1 = ((f32[16,64,128]{2,1,0:T(8,128)}), f32[16,64,128]{2,1,0:T(8,128)S(1)}, u32[]{:S(2)}, u32[]{:S(2)}) async-start(f32[16,64,128]{2,1,0:T(8,128)} %broadcast_in_dim.25), calls=%async_computation.1 | async-start | bytes 1048576 | tf_op jit(solution)/shard_map/all_to_all | solution.py:53
  39.7 4.2 collective-permute-start
  68.9 3.7 collective-permute-start.1
  120.0 4.1 collective-permute-start.2
  151.0 3.0 collective-permute-start.3
  202.8 3.9 collective-permute-start.4
  225.8 3.6 collective-permute-start.5
  277.1 4.1 collective-permute-start.6
  308.0 2.8 collective-permute-start.7
  359.6 4.2 collective-permute-start.8
  383.0 3.6 collective-permute-start.9
  434.0 4.1 collective-permute-start.10
  465.0 2.8 collective-permute-start.11
